TPU v7x, 32 devices: a whole 2x2x4 slice. The times are simulated.
32 devices in a mesh: groups: 2 (over y), ctx: 4 (over z), tp: 4 (over x, core).
Axes of the slice: x: 2, y: 2, z: 4, core: 2. Of those that a mesh axis runs over, the one named last changes fastest.
Arguments:
- query_rows: bfloat16 [1024, 4096], P(('groups', 'ctx'), 'tp'), parts along dimension 0, may hold values from -36 to 36
- key_rows: bfloat16 [1024, 1024], P(('groups', 'ctx'), 'tp'), parts along dimension 0, may hold values from -9 to 9
- value_rows: bfloat16 [1024, 1024], P(('groups', 'ctx'), 'tp'), parts along dimension 0, may hold values from -6 to 6
- residual: bfloat16 [1024, 4096], P(('groups', 'ctx'), 'tp'), parts along dimension 0, may hold values from -6 to 6
- out_weight: bfloat16 [4096, 4096], P('tp', 'ctx'), may hold values from -0.09375 to 0.09375
- norm_gain: bfloat16 [4096], P('tp'), may hold values from 0.099609375 to 1.8984375
- query_weight: bfloat16 [4096, 4096], P('tp', 'ctx'), may hold values from -0.09375 to 0.09375
- key_value_weight: bfloat16 [4096, 2048], P('tp', 'ctx'), may hold values from -0.09375 to 0.09375
- token_types: int32 [1024], P('groups'), parts along dimension 0, may hold values from 0 to 1
- keep_list: int32 [1024], P('groups'), parts along dimension 0, may hold values from 0 to 1, as said below
- position_ids: int32 [3, 1024], P(None, 'groups'), parts along dimension 1, may hold values from 0 to 511
Outputs:
- kept_resid: bfloat16 [256, 4096], P(('groups', 'ctx'), 'tp'), parts along dimension 0
- attended_three: bfloat16 [256, 4096], P(('groups', 'ctx'), 'tp'), parts along dimension 0
There are 2 independent parts, one for each index of `groups`. A program takes and returns all parts, laid end to end along the dimension named above; an argument that names none is the same for every part. Nothing has to cross between parts.
Inputs may be any that keep to these rules, and one draw needn't show every extreme that they name: keep_list is 0 at text tokens; exactly 128 tokens are text or kept, and all text tokens fit among them.
All inputs are finite; a program needn't handle non-finite values.
Results may differ from a plain program's by a relative error of at most 0.01.
Values may be sent and summed in bfloat16 or wider, within the bound.
A program may use at most 64 MiB of HBM per device.

v0:
```python
import math

import jax
import jax.numpy as jnp
from jax import lax
from jax.sharding import PartitionSpec as P

D = 4096
HD = 128
KEPT_DEV = 32


neg_large = -1e30


def rope_angles(positions):
    half_dim = HD // 2
    frequency = jnp.arange(half_dim, dtype=jnp.float32)
    inverse = jnp.exp(frequency * (-2.0 * math.log(1000000.0) / HD))
    section = jnp.where(
        frequency < HD // 8, 0, jnp.where(frequency < HD // 8 + 3 * HD // 16, 1, 2)
    ).astype(jnp.int32)
    chosen = jnp.take(positions, section, axis=0).astype(jnp.float32)
    return chosen.T * inverse[None, :]


def rotate(states, angles):
    half_dim = HD // 2
    cosine = jnp.cos(angles)[:, None, :]
    sine_part = jnp.sin(angles)[:, None, :]
    leading = states[..., :half_dim]
    trailing = states[..., half_dim:]
    return jnp.concatenate(
        [leading * cosine - trailing * sine_part, trailing * cosine + leading * sine_part], axis=-1
    )


def attend(queries, key_block, value_block):
    row_count = queries.shape[0]
    pair_local = key_block.shape[1] // HD
    group_size = queries.shape[1] // HD // pair_local
    grouped = queries.reshape(row_count, pair_local, group_size, HD)
    query_index = lax.axis_index("ctx") * row_count + jnp.arange(row_count, dtype=jnp.int32)
    score_scale = HD ** (-0.5)
    key_piece = lax.all_gather(key_block, "ctx", axis=0, tiled=True)
    value_piece = lax.all_gather(value_block, "ctx", axis=0, tiled=True)
    key_count = key_piece.shape[0]
    key_heads = key_piece.reshape(key_count, pair_local, HD)
    value_heads = value_piece.reshape(key_count, pair_local, HD)
    scores = (
        jnp.einsum("tkgd,nkd->kgtn", grouped, key_heads, preferred_element_type=jnp.float32)
        * score_scale
    )
    key_index = jnp.arange(key_count, dtype=jnp.int32)
    allowed = key_index[None, :] <= query_index[:, None]
    scores = jnp.where(allowed, scores, neg_large)
    running = jnp.full((pair_local, group_size, row_count), neg_large, jnp.float32)
    newest = jnp.maximum(running, jnp.max(scores, axis=-1))
    probs = jnp.where(allowed, jnp.exp(scores - newest[..., None]), 0.0)
    denominator = jnp.sum(probs, axis=-1)
    accum = jnp.einsum(
        "kgtn,nkd->kgtd",
        probs.astype(jnp.bfloat16),
        value_heads,
        preferred_element_type=jnp.float32,
    )
    running, denominator, accum = (newest, denominator, accum)
    result = accum / denominator[..., None]
    return result.transpose(2, 0, 1, 3).reshape(row_count, -1).astype(jnp.bfloat16)


def project(row_block, weights):
    row_total = row_block.shape[0]
    shard_count = lax.axis_size("ctx")
    tensor_count = lax.axis_size("tp")
    widths = [matrix.shape[1] for matrix in weights]
    width_sum = sum(widths)
    combined = weights[0] if len(weights) == 1 else jnp.concatenate(weights, axis=1)
    update = jnp.dot(
        row_block,
        lax.all_gather(combined, "ctx", axis=1, tiled=True),
        preferred_element_type=jnp.float32,
    )
    arranged = update.reshape(row_total, shard_count, width_sum)
    member_blocks = []
    offset = 0
    for width in widths:
        member = arranged[:, :, offset : offset + width].reshape(
            row_total, tensor_count, shard_count * width // tensor_count
        )
        member_blocks.append(member)
        offset += width
    stacked = jnp.concatenate(member_blocks, axis=2).reshape(row_total, -1)
    own_share = lax.psum_scatter(stacked, "tp", scatter_dimension=1, tiled=True)
    results = []
    offset = 0
    for width in widths:
        share_width = shard_count * width // tensor_count
        results.append(own_share[:, offset : offset + share_width])
        offset += share_width
    return results


def relocate(row_block, source, first_row):
    row_total = row_block.shape[0]
    shard_count = lax.axis_size("ctx")
    local_index = source - first_row
    present = (local_index >= 0) & (local_index < row_total)
    picked = jnp.take(row_block, jnp.clip(local_index, 0, row_total - 1), axis=0)
    outgoing = jnp.where(present[:, None], picked, jnp.zeros_like(picked))
    incoming = lax.all_to_all(outgoing, "ctx", split_axis=0, concat_axis=0, tiled=True)
    slot_count = incoming.shape[0] // shard_count
    return jnp.sum(
        incoming.reshape(shard_count, slot_count, -1).astype(jnp.float32), axis=0
    ).astype(jnp.bfloat16)


def on_device(
    query_rows,
    key_rows,
    value_rows,
    residual,
    out_weight,
    norm_gain,
    query_weight,
    key_value_weight,
    token_types,
    keep_list,
    position_ids,
):
    shard_count = lax.axis_size("ctx")
    shard_index = lax.axis_index("ctx")
    local_rows = query_rows.shape[0]
    kept_flags = ((token_types == 0) | (keep_list == 1)).astype(jnp.int32)
    running_count = jnp.cumsum(kept_flags)
    slot_numbers = jnp.arange(KEPT_DEV * shard_count, dtype=jnp.int32) + 1
    source = jnp.searchsorted(running_count, slot_numbers, side="left")
    attended = attend(query_rows, key_rows, value_rows)
    first_row = shard_index * local_rows
    summed = project(attended, [out_weight])[0]
    hidden = (residual.astype(jnp.float32) + summed).astype(jnp.bfloat16)
    kept_resid = relocate(hidden, source, first_row)
    squares = lax.psum(jnp.sum(jnp.square(kept_resid.astype(jnp.float32)), axis=1), "tp")
    normed = (
        kept_resid.astype(jnp.float32)
        * lax.rsqrt(squares[:, None] / D + 1e-06)
        * norm_gain.astype(jnp.float32)[None, :]
    ).astype(jnp.bfloat16)
    query_proj, pair_proj = project(normed, [query_weight, key_value_weight])
    kept_count = normed.shape[0]
    own_source = lax.dynamic_slice_in_dim(source, shard_index * kept_count, kept_count)
    angles = rope_angles(jnp.take(position_ids, own_source, axis=1))
    query_three = (
        rotate(query_proj.reshape(kept_count, -1, HD), angles)
        .reshape(kept_count, -1)
        .astype(jnp.bfloat16)
    )
    pair_heads = pair_proj.reshape(kept_count, -1, 2, HD)
    key_three = rotate(pair_heads[:, :, 0], angles).reshape(kept_count, -1).astype(jnp.bfloat16)
    value_three = pair_heads[:, :, 1].reshape(kept_count, -1).astype(jnp.bfloat16)
    return (kept_resid, attend(query_three, key_three, value_three))


def solution(mesh):
    in_specs = (
        P(("groups", "ctx"), "tp"),
        P(("groups", "ctx"), "tp"),
        P(("groups", "ctx"), "tp"),
        P(("groups", "ctx"), "tp"),
        P("tp", "ctx"),
        P("tp"),
        P("tp", "ctx"),
        P("tp", "ctx"),
        P("groups"),
        P("groups"),
        P(None, "groups"),
    )
    out_specs = (P(("groups", "ctx"), "tp"), P(("groups", "ctx"), "tp"))
    return jax.shard_map(
        on_device, mesh=mesh, in_specs=in_specs, out_specs=out_specs, check_vma=False
    )
```

profile of v0, /device:TPU:0, one launch (start us, length us, event | category | flops | bytes accessed | tf_op | source)
XLA Modules:
  0.0 488.9 jit_solution(13345286921516453069)
XLA Ops:
  7.2 0.7 all-gather.3.cloned.1.call-update
  8.0 15.9 %all_gather.19 = bf16[512,256]{1,0:T(8,128)(2,1)S(1)} all-gather(bf16[128,256]{1,0:T(8,128)(2,1)S(1)} %copy-done.5), channel_id=1, replica_groups=mesh['groups'=2,'ctx'=4,'tp'=4] {'ctx'}, dimensions={0}, use_global_device_ids=true | all-gather | bytes 327680 | tf_op jit(solution)/shard_map/all_gather | solution.py:46
  24.4 20.5 %all_gather.18 = bf16[512,256]{0,1:T(8,128)(2,1)S(1)} all-gather(bf16[128,256]{0,1:T(8,128)(2,1)S(1)} %copy.41), channel_id=1, replica_groups=mesh['groups'=2,'ctx'=4,'tp'=4] {'ctx'}, dimensions={0}, use_global_device_ids=true | all-gather | bytes 327680 | tf_op jit(solution)/shard_map/all_gather | solution.py:45
  46.7 119.4 %all-gather.3.cloned.1.call-done = bf16[1024,4096]{1,0:T(8,128)(2,1)} async-done(((bf16[1024,1024]{1,0:T(8,128)(2,1)}), bf16[1024,4096]{1,0:T(8,128)(2,1)}) %all-gather.3.cloned.1.call-update) | async-done | bytes 8388624 | tf_op jit(solution)/shard_map/all_gather | solution.py:81
  166.1 6.1 %fusion.40 = f32[128,4096]{1,0:T(8,128)} fusion(bf16[128,1024]{0,1:T(8,128)(2,1)S(1)} %bitcast.89, bf16[1024,4096]{1,0:T(8,128)(2,1)} %all-gather.3.cloned.1.call-done), kind=kOutput, calls=%fused_computation.93 | convolution fusion | flops 1073741824 | bytes 10747904 | tf_op jit(solution)/shard_map/dot_general | solution.py:79
  172.3 1.5 copy-done
  173.8 1.9 pad_maximum_fusion
  177.0 13.3 %while.24 = (s32[]{:T(128)}, u32[128]{0:T(128)S(1)}, u32[128]{0:T(128)S(1)}, s32[512]{0:T(512)S(1)}, s32[]{:T(128)}, /*index=5*/s32[]{:T(128)}, s32[]{}) while((s32[]{:T(128)}, u32[128]{0:T(128)S(1)}, u32[128]{0:T(128)S(1)}, s32[512]{0:T(512)S(1)}, s32[]{:T(128)}, /*index=5*/s32[]{:T(128)}, s32[]{}) %tuple.45), condition=%wide.region_3.4_spmd.clone, body=%wide.region_2.3_spmd.clone.sunk | while | flops 2820 | bytes 10348 | solution.py:137
  177.0 1.3 gather_fusion
  178.4 1.3 gather_fusion
  179.7 1.3 gather_fusion
  181.0 1.3 gather_fusion
  182.4 1.3 gather_fusion
  183.7 1.3 gather_fusion
  185.0 1.3 gather_fusion
  186.4 1.3 gather_fusion
  187.7 1.3 gather_fusion
  189.1 1.3 gather_fusion
  190.6 11.9 %reduce-scatter.3.cloned.1.call-done = f32[128,1024]{1,0:T(8,128)} async-done(((f32[128,4096]{1,0:T(8,128)}), f32[128,1024]{1,0:T(8,128)}) %reduce-scatter.3.cloned.1.call-update) | async-done | bytes 524304 | tf_op jit(solution)/shard_map/reduce_scatter | solution.py:94
  202.4 1.1 add_convert_fusion
  203.5 0.9 gather_fusion.1
  204.4 0.8 select_select_fusion
  205.2 4.6 all-to-all-start
  209.8 9.0 %all-to-all-done = bf16[4,32,1024]{2,1,0:T(8,128)(2,1)S(1)} async-done(((bf16[4,32,1024]{2,1,0:T(8,128)(2,1)}), bf16[4,32,1024]{2,1,0:T(8,128)(2,1)S(1)}, u32[]{:S(2)}, u32[]{:S(2)}) %all-to-all-start) | async-done | bytes 262176 | tf_op jit(solution)/shard_map/all_to_all | solution.py:111
  219.0 6.1 %psum.7 = f32[32]{0:T(128)S(1)} all-reduce(f32[32]{0:T(128)S(1)} %fusion.20), channel_id=1, replica_groups=mesh['groups'=2,'ctx'=4,'tp'=4] {'tp'}, use_global_device_ids=true, to_apply=%region_9.10 | all-reduce | flops 32 | bytes 256 | tf_op jit(solution)/shard_map/psum | solution.py:143
  225.1 197.3 %all-gather.5.cloned.1.call-done = bf16[1024,6144]{1,0:T(8,128)(2,1)} async-done(((bf16[1024,1536]{1,0:T(8,128)(2,1)}), bf16[1024,6144]{1,0:T(8,128)(2,1)}) %all-gather.5.cloned.1.call-update) | async-done | bytes 12582928 | tf_op jit(solution)/shard_map/all_gather | solution.py:81
  422.3 7.8 %fusion.26 = f32[32,6144]{1,0:T(8,128)} fusion(bf16[1024,6144]{1,0:T(8,128)(2,1)} %all-gather.5.cloned.1.call-done, bf16[32,1024]{1,0:T(8,128)(2,1)S(1)} %reduce_sum.40, f32[1024]{0:T(1024)S(1)} %convert_element_type.72, f32[32]{0:T(128)S(1)} %add_rsqrt_fusion), kind=kOutput, calls=%fused_computation.47 | convolution fusion | flops 402784256 | bytes 13439104 | tf_op jit(solution)/shard_map/dot_general | solution.py:79
  432.3 19.5 %reduce-scatter.5.cloned.1.call-done = f32[32,1536]{1,0:T(8,128)} async-done(((f32[32,6144]{1,0:T(8,128)}), f32[32,1536]{1,0:T(8,128)}) %reduce-scatter.5.cloned.1.call-update) | async-done | bytes 196624 | tf_op jit(solution)/shard_map/reduce_scatter | solution.py:94
  451.8 0.8 slice.53
  452.8 13.2 %all_gather.23 = bf16[128,256]{1,0:T(8,128)(2,1)S(1)} all-gather(bf16[32,256]{1,0:T(8,128)(2,1)S(1)} %bitcast.96), channel_id=1, replica_groups=mesh['groups'=2,'ctx'=4,'tp'=4] {'ctx'}, dimensions={0}, use_global_device_ids=true | all-gather | bytes 81920 | tf_op jit(solution)/shard_map/all_gather | solution.py:46
  466.4 13.2 %all_gather.22 = bf16[128,256]{1,0:T(8,128)(2,1)S(1)} all-gather(bf16[32,256]{1,0:T(8,128)(2,1)S(1)} %bitcast.97), channel_id=1, replica_groups=mesh['groups'=2,'ctx'=4,'tp'=4] {'ctx'}, dimensions={0}, use_global_device_ids=true | all-gather | bytes 81920 | tf_op jit(solution)/shard_map/all_gather | solution.py:45
  479.7 0.9 slice_bitcast_fusion
  (120 shorter events, 8.6 us)
Async XLA Ops:
  7.2 0.8 copy-start.5
  7.2 16.9 %copy-start.6 = (bf16[128,256]{1,0:T(8,128)(2,1)S(1)}, bf16[128,256]{1,0:T(8,128)(2,1)}, u32[]{:S(2)}) copy-start(bf16[128,256]{1,0:T(8,128)(2,1)} %param.14) | copy-start | bytes 196612
  7.2 17.0 %copy-start.3 = (bf16[128,1024]{1,0:T(8,128)(2,1)S(1)}, bf16[128,1024]{1,0:T(8,128)(2,1)}, u32[]{:S(2)}) copy-start(bf16[128,1024]{1,0:T(8,128)(2,1)} %param.13) | copy-start | bytes 786436
  7.2 158.9 %all-gather.3.cloned.1.call-start = ((), (), s32[]{:S(2)}) async-start(), calls=%async_computation.3 | async-start | bytes 10485760 | tf_op jit(solution)/shard_map/all_gather | solution.py:81
  7.9 194.5 %reduce-scatter.3.cloned.1.call-start = ((), (), s32[]{:S(2)}) async-start(), calls=%async_computation.4 | async-start | bytes 2621440 | tf_op jit(solution)/shard_map/reduce_scatter | solution.py:94
  166.1 6.2 %copy-start.1 = (bf16[1024,512]{1,0:T(8,128)(2,1)S(1)}, bf16[1024,512]{1,0:T(8,128)(2,1)}, u32[]{:S(2)}) copy-start(bf16[1024,512]{1,0:T(8,128)(2,1)} %param.20) | copy-start | bytes 3145732
  172.2 1.6 copy-start
  172.2 250.1 %all-gather.5.cloned.1.call-start = ((), (), s32[]{:S(2)}) async-start(), calls=%async_computation.5 | async-start | bytes 15728640 | tf_op jit(solution)/shard_map/all_gather | solution.py:81
  175.7 0.7 copy-start.8
  175.7 0.7 copy-start.9
  175.7 26.7 %copy-start.4 = (bf16[128,1024]{1,0:T(8,128)(2,1)S(1)}, bf16[128,1024]{1,0:T(8,128)(2,1)}, u32[]{:S(2)}) copy-start(bf16[128,1024]{1,0:T(8,128)(2,1)} %param.16) | copy-start | bytes 786436
  190.6 19.2 %copy-start.10 = (bf16[1024]{0:T(1024)(128)(2,1)S(1)}, bf16[1024]{0:T(1024)(128)(2,1)}, u32[]{:S(2)}) copy-start(bf16[1024]{0:T(1024)(128)(2,1)} %param.18) | copy-start | bytes 6148
  205.2 13.6 %all-to-all-start = ((bf16[4,32,1024]{2,1,0:T(8,128)(2,1)}), bf16[4,32,1024]{2,1,0:T(8,128)(2,1)S(1)}, u32[]{:S(2)}, u32[]{:S(2)}) async-start(bf16[4,32,1024]{2,1,0:T(8,128)(2,1)} %select_select_fusion), calls=%async_computation.1 | async-start | bytes 524288 | tf_op jit(solution)/shard_map/all_to_all | solution.py:111
  209.8 242.0 %reduce-scatter.5.cloned.1.call-start = ((), (), s32[]{:S(2)}) async-start(), calls=%async_computation.6 | async-start | bytes 983040 | tf_op jit(solution)/shard_map/reduce_scatter | solution.py:94
  218.9 211.3 %copy-start.2 = (bf16[32,1024]{1,0:T(8,128)(2,1)}, bf16[32,1024]{1,0:T(8,128)(2,1)S(1)}, u32[]{:S(2)}) copy-start(bf16[32,1024]{1,0:T(8,128)(2,1)S(1)} %reduce_sum.40) | copy-start | bytes 196612
  225.1 205.1 %copy-start.7 = (s32[3,512]{1,0:T(4,128)S(1)}, s32[3,512]{1,0:T(4,128)}, u32[]{:S(2)}) copy-start(s32[3,512]{1,0:T(4,128)} %param.23) | copy-start | bytes 18436
Sparse Core Ops, SparseCore 0:
  9.6 156.4 all-gather.2
  172.4 30.0 reduce-scatter.2
  204.1 218.2 all-gather.4
  430.3 21.4 reduce-scatter.4
where the time goes:
time: 489 us
  waiting for transfers between devices  358 us (73%)
  blocking collectives  68.9 us (14%)
  local copies, waits for them, and re-layouts  20.9 us (4%)
  matrix products  15.6 us (3%)
  between operations  14.1 us (3%)
  other arithmetic  6.39 us (1%)
    all_gather x2, waiting for transfers between devices, project(): lax.all_gather(combined, 'ctx', axis=1, tiled=True)  317 us
    all_gather x2, blocking collectives, attend(): key_piece = lax.all_gather(key_block, 'ctx', axis=0, tiled=True)  33.7 us
    reduce_scatter x2, waiting for transfers between devices, project(): own_share = lax.psum_scatter(stacked, 'tp', scatter_dimension=1, tiled=True)  31.4 us
    all_gather x2, blocking collectives, attend(): value_piece = lax.all_gather(value_block, 'ctx', axis=0, tiled=True)  29.2 us
    dot_general x2, matrix products, project(): jnp.dot(row_block, lax.all_gather(combined, 'ctx', axis=1, tiled=True), p...  13.9 us
    gather x10, local copies, waits for them, and re-layouts, on_device(): source = jnp.searchsorted(running_count, slot_numbers, side='left')  12.7 us
  transfers between devices with their start and end apart: 5, of which 5 were waited for; matrix products, arithmetic and copies ran while one was open for 5% of the time, Pallas kernels for 0%

commit v1 on v0

--- a/solution.py
+++ b/solution.py
@@ -3,6 +3,8 @@
 import jax
 import jax.numpy as jnp
 from jax import lax
+from jax.experimental import pallas as pl
+from jax.experimental.pallas import tpu as pltpu
 from jax.sharding import PartitionSpec as P
 
 D = 4096
@@ -160,6 +162,308 @@
     value_three = pair_heads[:, :, 1].reshape(kept_count, -1).astype(jnp.bfloat16)
     return (kept_resid, attend(query_three, key_three, value_three))
 
+MESH = pl.DeviceIdType.MESH
+N = 4
+
+
+def shifted(index, step):
+    return lax.rem(index + step, N)
+
+
+def block_of(index, size):
+    return pl.ds(pl.multiple_of(index * size, size), size)
+
+
+def softmax_pair(queries, keys, values, allowed):
+    scores = lax.dot_general(
+        queries, keys, (((1,), (1,)), ((), ())), preferred_element_type=jnp.float32
+    ) * (HD ** (-0.5))
+    scores = jnp.where(allowed, scores, neg_large)
+    probs = jnp.exp(scores - jnp.max(scores, axis=1, keepdims=True))
+    denominator = jnp.sum(probs, axis=1, keepdims=True)
+    gained = jnp.dot(probs.astype(jnp.bfloat16), values, preferred_element_type=jnp.float32)
+    return (gained / denominator).astype(jnp.bfloat16)
+
+
+def fused_kernel(
+    query_ref, key_ref, value_ref, resid_ref, out_w_ref, gain_ref, query_w_ref, pair_w_ref,
+    types_ref, keep_ref, pos_ref,
+    kept_out, att_out,
+    q_all, k_all, v_all, r_in, out_w, query_w, pair_w, pick, cos_s, sin_s,
+    att_all, part, part_b, part_in, hid_own, hid_all,
+    q_part, pair_part, sq_part, q_in, pair_in, sq_in, o_own, o_in,
+    w_sem, own_sem, s1, r1, s_res, r_res, s2, r2, s3, r3, s4, r4, s5, r5, s6, r6,
+):
+    g, c, t = lax.axis_index("groups"), lax.axis_index("ctx"), lax.axis_index("tp")
+    rows = query_ref.shape[0]
+    tokens = q_all.shape[0]
+    kept = pick.shape[0]
+    share = kept // N
+    f32, bf16 = jnp.float32, jnp.bfloat16
+
+    def send(source, target, s_sem, r_sem, cc, tt):
+        return pltpu.make_async_remote_copy(
+            src_ref=source, dst_ref=target, send_sem=s_sem, recv_sem=r_sem,
+            device_id=(g, cc, tt), device_id_type=MESH,
+        )
+
+    barrier = pltpu.get_barrier_semaphore()
+    for dc in range(N):
+        for dt in range(N):
+            if dc or dt:
+                pl.semaphore_signal(
+                    barrier, inc=1, device_id=(g, shifted(c, dc), shifted(t, dt)),
+                    device_id_type=MESH,
+                )
+    weights = [
+        pltpu.make_async_copy(a, b, w_sem.at[i])
+        for i, (a, b) in enumerate([(out_w_ref, out_w), (query_w_ref, query_w), (pair_w_ref, pair_w)])
+    ]
+    here = block_of(c, rows)
+    arrays = [(query_ref, q_all, 2 * HD, 1), (key_ref, k_all, HD, 2), (value_ref, v_all, HD, 2)]
+    own = [
+        pltpu.make_async_copy(a.at[:, block_of(c // div, width)], b.at[here], own_sem.at[i])
+        for i, (a, b, width, div) in enumerate(arrays)
+    ]
+    for copy in own:
+        copy.start()
+    pl.semaphore_wait(barrier, N * N - 1)
+
+    first = []
+    for d in (2, 1, 3):
+        to = shifted(c, d)
+        for i, (a, b, width, div) in enumerate(arrays):
+            first.append(send(
+                a.at[:, block_of(to // div, width)], b.at[here],
+                s1.at[3 * (d - 1) + i], r1.at[3 * (d - 1) + i], to, t,
+            ))
+            first[-1].start()
+    resid_copy = send(resid_ref, r_in, s_res, r_res, t, c)
+
+    @pl.when(t != c)
+    def _():
+        resid_copy.start()
+
+    resid_own = pltpu.make_async_copy(resid_ref, r_in, own_sem.at[3])
+
+    @pl.when(t == c)
+    def _():
+        resid_own.start()
+
+    for copy in weights:
+        copy.start()
+
+    flags = jnp.where((types_ref[...] == 0) | (keep_ref[...] == 1), 1.0, 0.0)
+    before = lax.broadcasted_iota(jnp.int32, (tokens, tokens), 0) <= lax.broadcasted_iota(
+        jnp.int32, (tokens, tokens), 1
+    )
+    counts = jnp.dot(
+        jnp.broadcast_to(flags, (16, tokens)).astype(bf16),
+        jnp.where(before, 1.0, 0.0).astype(bf16),
+        preferred_element_type=f32,
+    )[0:1]
+    place = lax.broadcasted_iota(jnp.int32, (kept, tokens), 0).astype(f32) + 1.0
+    chosen = jnp.where((counts == place) & (flags > 0.5), 1.0, 0.0)
+    pick[...] = chosen.astype(bf16)
+    token = lax.broadcasted_iota(jnp.int32, (kept, tokens), 1)
+    source = jnp.sum(chosen * token.astype(f32), axis=1, keepdims=True)
+    lane = lax.broadcasted_iota(jnp.int32, (1, HD), 1)
+    freq = lax.rem(lane, HD // 2).astype(f32)
+    inverse = jnp.exp(freq * (-2.0 * math.log(1000000.0) / HD))
+    at = [
+        jnp.sum(chosen * pos_ref[i : i + 1, :].astype(f32), axis=1, keepdims=True) for i in range(3)
+    ]
+    angle = jnp.where(freq < HD // 8, at[0], jnp.where(freq < HD // 8 + 3 * HD // 16, at[1], at[2]))
+    angle = angle * inverse
+    cos_s[...] = jnp.cos(angle)
+    sin_s[...] = jnp.where(lane < HD // 2, -1.0, 1.0) * jnp.sin(angle)
+    allowed = token.astype(f32) <= source
+    allowed = jnp.concatenate([allowed, allowed], axis=0)
+
+    for copy in own:
+        copy.wait()
+    for copy in first:
+        copy.wait_recv()
+    queries = jnp.dot(pick[...], q_all[...], preferred_element_type=f32).astype(bf16)
+    queries = jnp.concatenate([queries[:, :HD], queries[:, HD:]], axis=0)
+    attended = softmax_pair(queries, k_all[...], v_all[...], allowed)
+    att_all[c, :, :HD] = attended[:kept]
+    att_all[c, :, HD:] = attended[kept:]
+
+    second = []
+    for d in (2, 1, 3):
+        second.append(send(att_all.at[c], att_all.at[c], s2.at[d - 1], r2.at[d - 1], shifted(c, d), t))
+        second[-1].start()
+
+    @pl.when(t != c)
+    def _():
+        resid_copy.wait_recv()
+
+    @pl.when(t == c)
+    def _():
+        resid_own.wait()
+
+    weights[0].wait()
+    part[...] = jnp.dot(pick[:, block_of(t, rows)], r_in[...], preferred_element_type=f32)
+    part[...] += jnp.dot(att_all[c], out_w[block_of(c, 2 * HD), :], preferred_element_type=f32)
+    for copy, d in zip(second, (2, 1, 3)):
+        copy.wait_recv()
+    for d in (1, 3, 2):
+        other = shifted(c, N - d)
+        part[...] += jnp.dot(att_all[other], out_w[block_of(other, 2 * HD), :], preferred_element_type=f32)
+    part_b[...] = part[...].astype(bf16)
+
+    third = []
+    for d in (2, 3, 1):
+        to = shifted(t, d)
+        third.append(send(part_b.at[block_of(to, share)], part_in.at[d - 1], s3.at[d - 1], r3.at[d - 1], c, to))
+        third[-1].start()
+    hidden = part[block_of(t, share), :]
+    for copy in third:
+        copy.wait_recv()
+    for d in range(N - 1):
+        hidden = hidden + part_in[d].astype(f32)
+    hid_own[...] = hidden.astype(bf16)
+
+    fourth = []
+    for d in range(N):
+        to = shifted(c, d)
+        fourth.append(send(hid_own, hid_all.at[t], s4.at[d], r4.at[t], to, c))
+    for d in (2, 1, 3):
+        fourth[d].start()
+
+    @pl.when(t != c)
+    def _():
+        fourth[0].start()
+
+    @pl.when(t == c)
+    def _():
+        hid_all[t] = hid_own[...]
+
+    weights[1].wait()
+    weights[2].wait()
+    for k in range(N):
+        @pl.when((t != c) | (t != k))
+        def _(k=k):
+            send(hid_own, hid_all.at[k], s4.at[k], r4.at[k], c, t).wait_recv()
+
+    kept_out[...] = hid_all[c]
+    resid = hid_all[...].reshape(kept, hid_all.shape[2]).astype(f32)
+    scaled = (resid * gain_ref[...].astype(f32)).astype(bf16)
+    squares = jnp.sum(jnp.square(resid), axis=1, keepdims=True)
+    sq_part[...] = jnp.broadcast_to(squares, (kept, HD)).T[:8]
+    projected = jnp.dot(scaled, query_w[...], preferred_element_type=f32).astype(bf16)
+    for i in range(N):
+        q_part[i] = projected[:, 2 * HD * i : 2 * HD * (i + 1)]
+    projected = jnp.dot(scaled, pair_w[...], preferred_element_type=f32).astype(bf16)
+    for i in range(2):
+        pair_part[i] = projected[:, 2 * HD * i : 2 * HD * (i + 1)]
+
+    fifth = []
+    for d in (2, 3, 1):
+        to = shifted(t, d)
+        for i, (a, b) in enumerate([
+            (q_part.at[to], q_in.at[d - 1]), (pair_part.at[to // 2], pair_in.at[d - 1]),
+            (sq_part, sq_in.at[d - 1]),
+        ]):
+            fifth.append(send(a, b, s5.at[3 * (d - 1) + i], r5.at[3 * (d - 1) + i], c, to))
+            fifth[-1].start()
+    query = q_part[t].astype(f32)
+    pair = pair_part[t // 2].astype(f32)
+    squares = sq_part[...]
+    for copy in fifth:
+        copy.wait_recv()
+    for d in range(N - 1):
+        query = query + q_in[d].astype(f32)
+        pair = pair + pair_in[d].astype(f32)
+        squares = squares + sq_in[d]
+    total = jnp.broadcast_to(squares[0:1], (kept, HD)).T
+    scale = lax.rsqrt(total / D + 1e-06)
+    cosine, sine = cos_s[...] * scale, sin_s[...] * scale
+
+    def turned(head):
+        return (head * cosine + pltpu.roll(head, HD // 2, 1) * sine).astype(bf16)
+
+    queries = jnp.concatenate([turned(query[:, :HD]), turned(query[:, HD:])], axis=0)
+    row = lax.broadcasted_iota(jnp.int32, (kept, kept), 0)
+    column = lax.broadcasted_iota(jnp.int32, (kept, kept), 1)
+    causal = column <= row
+    causal = jnp.concatenate([causal, causal], axis=0)
+    values = (pair[:, HD:] * scale).astype(bf16)
+    attended = softmax_pair(queries, turned(pair[:, :HD]), values, causal)
+    o_own[:, :HD] = attended[:kept]
+    o_own[:, HD:] = attended[kept:]
+
+    sixth = []
+    for d in range(N):
+        to = shifted(c, d)
+        sixth.append(send(o_own.at[block_of(to, share)], o_in.at[t], s6.at[d], r6.at[t], to, c))
+    for d in (2, 1, 3):
+        sixth[d].start()
+
+    @pl.when(t != c)
+    def _():
+        sixth[0].start()
+
+    @pl.when(t == c)
+    def _():
+        o_in[t] = o_own[block_of(c, share), :]
+
+    for copies in (first, second, third, fifth, fourth[1:], sixth[1:]):
+        for copy in copies:
+            copy.wait_send()
+
+    @pl.when(t != c)
+    def _():
+        resid_copy.wait_send()
+        fourth[0].wait_send()
+        sixth[0].wait_send()
+
+    for k in range(N):
+        @pl.when((t != c) | (t != k))
+        def _(k=k):
+            send(o_own.at[block_of(c, share)], o_in.at[k], s6.at[k], r6.at[k], c, t).wait_recv()
+
+        att_out[:, 2 * HD * k : 2 * HD * (k + 1)] = o_in[k]
+
+
+def fused(
+    query_rows, key_rows, value_rows, residual, out_weight, norm_gain, query_weight,
+    key_value_weight, token_types, keep_list, position_ids,
+):
+    rows, width = query_rows.shape
+    tokens = rows * N
+    kept = KEPT_DEV * N
+    bf16, f32 = jnp.bfloat16, jnp.float32
+    dma = pltpu.SemaphoreType.DMA
+    vmem, anywhere = pl.BlockSpec(memory_space=pltpu.VMEM), pl.BlockSpec(memory_space=pl.ANY)
+    scratch = [
+        ((tokens, 2 * HD), bf16), ((tokens, HD), bf16), ((tokens, HD), bf16), (residual.shape, bf16),
+        (out_weight.shape, bf16), (query_weight.shape, bf16), (key_value_weight.shape, bf16),
+        ((kept, tokens), bf16), ((kept, HD), f32), ((kept, HD), f32),
+        ((N, kept, 2 * HD), bf16), ((kept, width), f32), ((kept, width), bf16),
+        ((N - 1, KEPT_DEV, width), bf16), ((KEPT_DEV, width), bf16), ((N, KEPT_DEV, width), bf16),
+        ((N, kept, 2 * HD), bf16), ((2, kept, 2 * HD), bf16), ((8, HD), f32),
+        ((N - 1, kept, 2 * HD), bf16), ((N - 1, kept, 2 * HD), bf16), ((N - 1, 8, HD), f32),
+        ((kept, 2 * HD), bf16), ((N, KEPT_DEV, 2 * HD), bf16),
+    ]
+    counts = [(3,), (4,), (9,), (9,), (), (), (3,), (3,), (3,), (3,), (4,), (4,), (9,), (9,), (4,), (4,)]
+    return pl.pallas_call(
+        fused_kernel,
+        out_shape=[jax.ShapeDtypeStruct((KEPT_DEV, width), bf16)] * 2,
+        in_specs=[anywhere] * 5 + [vmem] + [anywhere] * 2 + [vmem] * 3,
+        out_specs=[vmem, vmem],
+        scratch_shapes=[pltpu.VMEM(s, d) for s, d in scratch]
+        + [dma(n) if n else dma for n in counts],
+        compiler_params=pltpu.CompilerParams(
+            collective_id=0, has_side_effects=True, vmem_limit_bytes=48 * 1024 * 1024
+        ),
+    )(
+        query_rows, key_rows, value_rows, residual, out_weight, norm_gain.reshape(1, -1),
+        query_weight, key_value_weight, token_types.reshape(1, -1), keep_list.reshape(1, -1),
+        position_ids,
+    )
+
 
 def solution(mesh):
     in_specs = (
@@ -176,6 +480,7 @@
         P(None, "groups"),
     )
     out_specs = (P(("groups", "ctx"), "tp"), P(("groups", "ctx"), "tp"))
+    whole_heads = mesh.shape["ctx"] == N and mesh.shape["tp"] == N
     return jax.shard_map(
-        on_device, mesh=mesh, in_specs=in_specs, out_specs=out_specs, check_vma=False
-    )
+        fused if whole_heads else on_device, mesh=mesh, in_specs=in_specs, out_specs=out_specs, check_vma=False
+    )

time: 489 us -> 69.7 us (0.14)
  waiting for transfers between devices: 358 us -> 0 us
  blocking collectives: 68.9 us -> 0 us
  Pallas kernels: 0 us -> 56.1 us
  matrix products: 15.6 us -> 0 us
  between operations: 14.1 us -> 0.65 us
  local copies, waits for them, and re-layouts: 20.9 us -> 12 us
  other arithmetic: 6.39 us -> 0 us
    all_gather x2 -> x0, waiting for transfers between devices: 317 us -> none  [project(): lax.all_gather(combined, 'ctx', axis=1, tiled=True)]
    all_gather x4 -> x0, blocking collectives: 62.9 us -> none  [the longest x2 33.7 us: attend(): key_piece = lax.all_gather(key_block, 'ctx', axis=0, tiled=True)]
    pallas_call x0 -> x1, Pallas kernels: none -> 56.1 us  [fused(): pl.pallas_call(fused_kernel, out_shape=[jax.ShapeDtypeStruct((KEPT_DEV, w...]
    reduce_scatter x2 -> x0, waiting for transfers between devices: 31.4 us -> none  [project(): own_share = lax.psum_scatter(stacked, 'tp', scatter_dimension=1, tiled=True)]
    dot_general x6 -> x0, matrix products: 15.6 us -> none  [the longest x2 13.9 us: project(): jnp.dot(row_block, lax.all_gather(combined, 'ctx', axis=1, tiled=True), p...]
    gather x13 -> x0, local copies, waits for them, and re-layouts: 14.7 us -> none  [the longest x10 12.7 us: on_device(): source = jnp.searchsorted(running_count, slot_numbers, side='left')]
    all_to_all x1 -> x0, waiting for transfers between devices: 9.02 us -> none  [relocate(): lax.all_to_all(outgoing, 'ctx', split_axis=0, concat_axis=0, tiled=True)]
    unnamed x29 -> x22, local copies, waits for them, and re-layouts: 3.45 us -> 11.3 us
  transfers between devices with their start and end apart: 5 -> 0, of which waited for: 5 -> 0; matrix products, arithmetic and copies ran while one was open for 5% -> 0% of each run, Pallas kernels for 0% -> 0%
where the time goes in v1:
time: 69.7 us; the launch traced here: 68.7 us
  Pallas kernels  56.1 us (80%)
  local copies, waits for them, and re-layouts  12 us (17%)
    pallas_call x1, Pallas kernels, fused(): pl.pallas_call(fused_kernel, out_shape=[jax.ShapeDtypeStruct((KEPT_DEV, w...  56.1 us
    unnamed x22, local copies, waits for them, and re-layouts  11.3 us

profile of v1, /device:TPU:0, one launch (start us, length us, event | category | flops | bytes accessed | tf_op | source)
XLA Modules:
  0.0 68.7 jit_solution(3434087538788744255)
XLA Ops:
  0.6 0.7 reshape.13.gain_ref
  1.3 0.0 copy-start
  1.3 1.6 %copy-done = bf16[1024,1024]{1,0:T(8,128)(2,1)S(1)} copy-done((bf16[1024,1024]{1,0:T(8,128)(2,1)S(1)}, bf16[1024,1024]{1,0:T(8,128)(2,1)}, u32[]{:S(2)}) %copy-start) | copy-done | bytes 2097176
  2.9 0.0 copy-start.1
  2.9 1.6 %copy-done.1 = bf16[1024,1024]{1,0:T(8,128)(2,1)S(1)} copy-done((bf16[1024,1024]{1,0:T(8,128)(2,1)S(1)}, bf16[1024,1024]{1,0:T(8,128)(2,1)}, u32[]{:S(2)}) %copy-start.1) | copy-done | bytes 2097176
  4.5 0.0 copy-start.2
  4.5 1.2 %copy-done.2 = bf16[1024,512]{1,0:T(8,128)(2,1)S(1)} copy-done((bf16[1024,512]{1,0:T(8,128)(2,1)S(1)}, bf16[1024,512]{1,0:T(8,128)(2,1)}, u32[]{:S(2)}) %copy-start.2) | copy-done | bytes 1048600
  5.7 0.0 copy-start.3
  5.7 0.9 %copy-done.3 = bf16[128,1024]{1,0:T(8,128)(2,1)S(1)} copy-done((bf16[128,1024]{1,0:T(8,128)(2,1)S(1)}, bf16[128,1024]{1,0:T(8,128)(2,1)}, u32[]{:S(2)}) %copy-start.3) | copy-done | bytes 262168
  6.7 0.0 copy-start.4
  6.7 0.9 %copy-done.4 = bf16[128,1024]{1,0:T(8,128)(2,1)S(1)} copy-done((bf16[128,1024]{1,0:T(8,128)(2,1)S(1)}, bf16[128,1024]{1,0:T(8,128)(2,1)}, u32[]{:S(2)}) %copy-start.4) | copy-done | bytes 262168
  7.6 0.0 copy-start.5
  7.6 0.8 %copy-done.5 = bf16[128,256]{1,0:T(8,128)(2,1)S(1)} copy-done((bf16[128,256]{1,0:T(8,128)(2,1)S(1)}, bf16[128,256]{1,0:T(8,128)(2,1)}, u32[]{:S(2)}) %copy-start.5) | copy-done | bytes 65560
  8.5 0.0 copy-start.6
  8.5 0.8 %copy-done.6 = bf16[128,256]{1,0:T(8,128)(2,1)S(1)} copy-done((bf16[128,256]{1,0:T(8,128)(2,1)S(1)}, bf16[128,256]{1,0:T(8,128)(2,1)}, u32[]{:S(2)}) %copy-start.6) | copy-done | bytes 65560
  9.3 0.0 copy-start.7
  9.3 0.7 %copy-done.7 = s32[3,512]{1,0:T(4,128)S(1)} copy-done((s32[3,512]{1,0:T(4,128)S(1)}, s32[3,512]{1,0:T(4,128)}, u32[]{:S(2)}) %copy-start.7) | copy-done | bytes 6168
  10.0 0.0 copy-start.8
  10.0 0.7 copy-done.8
  10.7 0.0 copy-start.9
  10.7 0.7 copy-done.9
  11.4 56.1 %shard_map.122 = (bf16[32,1024]{1,0:T(8,128)(2,1)S(1)}, bf16[32,1024]{1,0:T(8,128)(2,1)S(1)}) custom-call(bf16[128,1024]{1,0:T(8,128)(2,1)S(1)} %copy-done.3, bf16[128,256]{1,0:T(8,128)(2,1)S(1)} %copy-done.5, bf16[128,256]{1,0:T(8,128)(2,1)S(1)} %copy-done.6, bf16[128,1024]{1,0:T(8,128)(2,1)S(1)} %copy-done.4, bf16[1024,1024]{1,0:T(8,128)(2,1)S(1)} %copy-done, ...), custom_call_target="tpu_custom_call" | custom-call | tf_op jit(solution)/shard_map/pallas_call | solution.py:451
  67.4 0.6 copy.15
  68.1 0.6 copy.16
Async XLA Ops:
  1.3 1.6 %copy-start = (bf16[1024,1024]{1,0:T(8,128)(2,1)S(1)}, bf16[1024,1024]{1,0:T(8,128)(2,1)}, u32[]{:S(2)}) copy-start(bf16[1024,1024]{1,0:T(8,128)(2,1)} %out_w_ref.1) | copy-start | bytes 6291460
  2.9 1.6 %copy-start.1 = (bf16[1024,1024]{1,0:T(8,128)(2,1)S(1)}, bf16[1024,1024]{1,0:T(8,128)(2,1)}, u32[]{:S(2)}) copy-start(bf16[1024,1024]{1,0:T(8,128)(2,1)} %query_w_ref.1) | copy-start | bytes 6291460
  4.5 1.2 %copy-start.2 = (bf16[1024,512]{1,0:T(8,128)(2,1)S(1)}, bf16[1024,512]{1,0:T(8,128)(2,1)}, u32[]{:S(2)}) copy-start(bf16[1024,512]{1,0:T(8,128)(2,1)} %pair_w_ref.1) | copy-start | bytes 3145732
  5.7 0.9 %copy-start.3 = (bf16[128,1024]{1,0:T(8,128)(2,1)S(1)}, bf16[128,1024]{1,0:T(8,128)(2,1)}, u32[]{:S(2)}) copy-start(bf16[128,1024]{1,0:T(8,128)(2,1)} %query_ref.1) | copy-start | bytes 786436
  6.7 0.9 %copy-start.4 = (bf16[128,1024]{1,0:T(8,128)(2,1)S(1)}, bf16[128,1024]{1,0:T(8,128)(2,1)}, u32[]{:S(2)}) copy-start(bf16[128,1024]{1,0:T(8,128)(2,1)} %resid_ref.1) | copy-start | bytes 786436
  7.6 0.8 %copy-start.5 = (bf16[128,256]{1,0:T(8,128)(2,1)S(1)}, bf16[128,256]{1,0:T(8,128)(2,1)}, u32[]{:S(2)}) copy-start(bf16[128,256]{1,0:T(8,128)(2,1)} %key_ref.1) | copy-start | bytes 196612
  8.5 0.8 %copy-start.6 = (bf16[128,256]{1,0:T(8,128)(2,1)S(1)}, bf16[128,256]{1,0:T(8,128)(2,1)}, u32[]{:S(2)}) copy-start(bf16[128,256]{1,0:T(8,128)(2,1)} %value_ref.1) | copy-start | bytes 196612
  9.3 0.7 %copy-start.7 = (s32[3,512]{1,0:T(4,128)S(1)}, s32[3,512]{1,0:T(4,128)}, u32[]{:S(2)}) copy-start(s32[3,512]{1,0:T(4,128)} %pos_ref.1) | copy-start | bytes 18436
  10.0 0.7 copy-start.8
  10.7 0.7 copy-start.9

commit v2 on v1

--- a/solution.py
+++ b/solution.py
@@ -187,11 +187,12 @@
 
 def fused_kernel(
     query_ref, key_ref, value_ref, resid_ref, out_w_ref, gain_ref, query_w_ref, pair_w_ref,
-    types_ref, keep_ref, pos_ref,
-    kept_out, att_out,
+    types_hbm, keep_hbm, pos_hbm,
+    out_ref,
     q_all, k_all, v_all, r_in, out_w, query_w, pair_w, pick, cos_s, sin_s,
     att_all, part, part_b, part_in, hid_own, hid_all,
     q_part, pair_part, sq_part, q_in, pair_in, sq_in, o_own, o_in,
+    types_ref, keep_ref, pos_ref,
     w_sem, own_sem, s1, r1, s_res, r_res, s2, r2, s3, r3, s4, r4, s5, r5, s6, r6,
 ):
     g, c, t = lax.axis_index("groups"), lax.axis_index("ctx"), lax.axis_index("tp")
@@ -225,7 +226,11 @@
         pltpu.make_async_copy(a.at[:, block_of(c // div, width)], b.at[here], own_sem.at[i])
         for i, (a, b, width, div) in enumerate(arrays)
     ]
-    for copy in own:
+    small = [
+        pltpu.make_async_copy(a, b, own_sem.at[4 + i])
+        for i, (a, b) in enumerate([(types_hbm, types_ref), (keep_hbm, keep_ref), (pos_hbm, pos_ref)])
+    ]
+    for copy in own + small:
         copy.start()
     pl.semaphore_wait(barrier, N * N - 1)
 
@@ -253,6 +258,8 @@
     for copy in weights:
         copy.start()
 
+    for copy in small:
+        copy.wait()
     flags = jnp.where((types_ref[...] == 0) | (keep_ref[...] == 1), 1.0, 0.0)
     before = lax.broadcasted_iota(jnp.int32, (tokens, tokens), 0) <= lax.broadcasted_iota(
         jnp.int32, (tokens, tokens), 1
@@ -347,27 +354,30 @@
         def _(k=k):
             send(hid_own, hid_all.at[k], s4.at[k], r4.at[k], c, t).wait_recv()
 
-    kept_out[...] = hid_all[c]
+    out_ref[0] = hid_all[c]
     resid = hid_all[...].reshape(kept, hid_all.shape[2]).astype(f32)
-    scaled = (resid * gain_ref[...].astype(f32)).astype(bf16)
+    scaled = (resid * gain_ref[...].astype(f32).reshape(1, -1)).astype(bf16)
     squares = jnp.sum(jnp.square(resid), axis=1, keepdims=True)
     sq_part[...] = jnp.broadcast_to(squares, (kept, HD)).T[:8]
+    projected = jnp.dot(scaled, pair_w[...], preferred_element_type=f32).astype(bf16)
+    for i in range(2):
+        pair_part[i] = projected[:, 2 * HD * i : 2 * HD * (i + 1)]
+
+    fifth = []
+
+    def start_fifth(i, array, target):
+        for d in (2, 3, 1):
+            to = shifted(t, d)
+            at = 3 * (d - 1) + i
+            fifth.append(send(array(to), target.at[d - 1], s5.at[at], r5.at[at], c, to))
+            fifth[-1].start()
+
+    start_fifth(1, lambda to: pair_part.at[to // 2], pair_in)
+    start_fifth(2, lambda to: sq_part, sq_in)
     projected = jnp.dot(scaled, query_w[...], preferred_element_type=f32).astype(bf16)
     for i in range(N):
         q_part[i] = projected[:, 2 * HD * i : 2 * HD * (i + 1)]
-    projected = jnp.dot(scaled, pair_w[...], preferred_element_type=f32).astype(bf16)
-    for i in range(2):
-        pair_part[i] = projected[:, 2 * HD * i : 2 * HD * (i + 1)]
-
-    fifth = []
-    for d in (2, 3, 1):
-        to = shifted(t, d)
-        for i, (a, b) in enumerate([
-            (q_part.at[to], q_in.at[d - 1]), (pair_part.at[to // 2], pair_in.at[d - 1]),
-            (sq_part, sq_in.at[d - 1]),
-        ]):
-            fifth.append(send(a, b, s5.at[3 * (d - 1) + i], r5.at[3 * (d - 1) + i], c, to))
-            fifth[-1].start()
+    start_fifth(0, lambda to: q_part.at[to], q_in)
     query = q_part[t].astype(f32)
     pair = pair_part[t // 2].astype(f32)
     squares = sq_part[...]
@@ -424,7 +434,7 @@
         def _(k=k):
             send(o_own.at[block_of(c, share)], o_in.at[k], s6.at[k], r6.at[k], c, t).wait_recv()
 
-        att_out[:, 2 * HD * k : 2 * HD * (k + 1)] = o_in[k]
+        out_ref[1, :, 2 * HD * k : 2 * HD * (k + 1)] = o_in[k]
 
 
 def fused(
@@ -446,23 +456,25 @@
         ((N, kept, 2 * HD), bf16), ((2, kept, 2 * HD), bf16), ((8, HD), f32),
         ((N - 1, kept, 2 * HD), bf16), ((N - 1, kept, 2 * HD), bf16), ((N - 1, 8, HD), f32),
         ((kept, 2 * HD), bf16), ((N, KEPT_DEV, 2 * HD), bf16),
+        ((1, tokens), jnp.int32), ((1, tokens), jnp.int32), ((3, tokens), jnp.int32),
     ]
-    counts = [(3,), (4,), (9,), (9,), (), (), (3,), (3,), (3,), (3,), (4,), (4,), (9,), (9,), (4,), (4,)]
-    return pl.pallas_call(
+    counts = [(3,), (7,), (9,), (9,), (), (), (3,), (3,), (3,), (3,), (4,), (4,), (9,), (9,), (4,), (4,)]
+    both = pl.pallas_call(
         fused_kernel,
-        out_shape=[jax.ShapeDtypeStruct((KEPT_DEV, width), bf16)] * 2,
-        in_specs=[anywhere] * 5 + [vmem] + [anywhere] * 2 + [vmem] * 3,
-        out_specs=[vmem, vmem],
+        out_shape=jax.ShapeDtypeStruct((2, KEPT_DEV, width), bf16),
+        in_specs=[anywhere] * 5 + [vmem] + [anywhere] * 5,
+        out_specs=vmem,
         scratch_shapes=[pltpu.VMEM(s, d) for s, d in scratch]
         + [dma(n) if n else dma for n in counts],
         compiler_params=pltpu.CompilerParams(
-            collective_id=0, has_side_effects=True, vmem_limit_bytes=48 * 1024 * 1024
+            collective_id=0, has_side_effects=True, vmem_limit_bytes=62 * 1024 * 1024
         ),
     )(
-        query_rows, key_rows, value_rows, residual, out_weight, norm_gain.reshape(1, -1),
+        query_rows, key_rows, value_rows, residual, out_weight, norm_gain,
         query_weight, key_value_weight, token_types.reshape(1, -1), keep_list.reshape(1, -1),
         position_ids,
     )
+    return both[0], both[1]
 
 
 def solution(mesh):

time: 69.7 us -> 60.5 us (0.87)
  local copies, waits for them, and re-layouts: 12 us -> 1.53 us
  Pallas kernels: 56.1 us -> 57.7 us
    unnamed x22 -> x0, local copies, waits for them, and re-layouts: 11.3 us -> none
    pallas_call x1, Pallas kernels: 56.1 us -> 57.7 us  [fused(): pl.pallas_call(fused_kernel, out_shape=jax.ShapeDtypeStruct((2, KEPT_DEV,...]
    squeeze x0 -> x1, local copies, waits for them, and re-layouts: none -> 1.53 us  [fused(): return (both[0], both[1])]
where the time goes in v2:
time: 60.5 us; the launch traced here: 59.8 us
  Pallas kernels  57.7 us (95%)
  local copies, waits for them, and re-layouts  1.53 us (3%)
  between operations  0.64 us (1%)
    pallas_call x1, Pallas kernels, fused(): pl.pallas_call(fused_kernel, out_shape=jax.ShapeDtypeStruct((2, KEPT_DEV,...  57.7 us
    squeeze x1, local copies, waits for them, and re-layouts, fused(): return (both[0], both[1])  1.53 us

profile of v2, /device:TPU:0, one launch (start us, length us, event | category | flops | bytes accessed | tf_op | source)
XLA Modules:
  0.0 59.8 jit_solution(14995629906341215194)
XLA Ops:
  0.6 57.7 %shard_map.122 = bf16[2,32,1024]{2,1,0:T(8,128)(2,1)} custom-call(bf16[128,1024]{1,0:T(8,128)(2,1)} %query_ref.1, bf16[128,256]{1,0:T(8,128)(2,1)} %key_ref.1, bf16[128,256]{1,0:T(8,128)(2,1)} %value_ref.1, bf16[128,1024]{1,0:T(8,128)(2,1)} %resid_ref.1, bf16[1024,1024]{1,0:T(8,128)(2,1)} %out_w_ref.1, bf16[1024]{0:T(1024)(128)(2,1)} %gain_ref.1, ...), custom_call_target="tpu_custom_call" | custom-call | tf_op jit(solution)/shard_map/pallas_call | solution.py:462
  58.3 1.5 %slice_bitcast_fusion = (bf16[32,1024]{1,0:T(8,128)(2,1)}, bf16[32,1024]{1,0:T(8,128)(2,1)}) fusion(bf16[2,32,1024]{2,1,0:T(8,128)(2,1)} %shard_map.122), kind=kLoop, calls=%fused_computation | loop fusion | bytes 262144 | tf_op jit(solution)/shard_map/squeeze | solution.py:477
